TPU v7x, 32 devices: a whole 2x2x4 slice. The times are simulated.
32 devices in a mesh: level: 8 (over z, x), sample: 4 (over y, core).
Axes of the slice: x: 2, y: 2, z: 4, core: 2. Of those that a mesh axis runs over, the one named last changes fastest.
Arguments:
- samples: bfloat16 [32768, 512], P('level', 'sample'), may hold values from -6 to 6
- sketch: bfloat16 [2, 128, 256], replicated, may hold values from -0.375 to 0.375
Outputs:
- far_factors: float32 [128, 128, 128], P('level')
- near_factors: float32 [64, 128, 128], P('level')
- basis_rows: float32 [8192, 512], P('level', 'sample')
All inputs are finite; a program needn't handle non-finite values.
Results may differ from a plain program's by a relative error of at most 0.0031.
Values may be sent and summed in bfloat16 or wider, within the bound.
A program may use at most 64 MiB of HBM per device.

v0:
```python
import functools
import math

import jax
import jax.numpy as jnp
from jax import lax
from jax.experimental import pallas as pl
from jax.experimental.pallas import tpu as pltpu
from jax.sharding import PartitionSpec as P

SAMPLES = 512
RANK = 128
PANEL = 8
F32 = jnp.float32
BF16 = jnp.bfloat16


def split(value):
    high = value.astype(BF16).astype(F32)
    return high, value - high


def project_kernel(
    which, distance, group, relayed, rows_ref, sketch_ref, z_ref, gram_ref,
    kept, relay, arrived, part, first, partial, second, third, kept_sem,
    own_send, row_recv, outer_recv, inner_recv, outer_pass, inner_pass,
    first_send, first_recv, second_send, second_recv, third_send, third_recv,
):
    level, sample = lax.axis_index("level"), lax.axis_index("sample")
    upper = level // distance % 2
    other = level + distance - 2 * distance * upper
    core = sample % 2
    mate = sample + 1 - 2 * core
    across = sample + 2 - 4 * (sample // 2 % 2)
    count = arrived.shape[0]
    boxes = count // RANK
    chunks = boxes // group
    half = group // 2
    size = group * RANK
    if relayed:
        hop = distance // 2
        place = level // hop % 4
        inner = (place + 1) // 2 % 2
        beside = level + hop * (1 - 2 * (place % 2))
        cross = level + hop * (3 - 2 * place)
        targets = ({"level": beside}, {"level": cross}, {"sample": mate}, {"sample": across})
    else:
        targets = ({"level": other}, {"sample": mate}, {"sample": across})

    keep = pltpu.make_async_copy(
        rows_ref.at[pl.ds(pl.multiple_of(upper * count, size), count)], kept, kept_sem
    )
    keep.start()
    barrier = pltpu.get_barrier_semaphore()
    for target in targets:
        pl.semaphore_signal(barrier, inc=1, device_id=target, device_id_type=pl.DeviceIdType.MESH)
    pl.semaphore_wait(barrier, len(targets))

    def remote(src, dst, send, recv, c, target):
        return pltpu.make_async_remote_copy(
            src_ref=src, dst_ref=dst, send_sem=send.at[c], recv_sem=recv.at[c],
            device_id=target, device_id_type=pl.DeviceIdType.MESH,
        )

    def given(c):
        return rows_ref.at[pl.ds(pl.multiple_of((1 - upper) * count + c * size, size), size)]

    def at(c):
        return pl.ds(c * size, size)

    if relayed:
        outward = [
            remote(given(c), relay.at[0, at(c)], own_send, outer_recv, c, {"level": beside})
            for c in range(chunks)
        ]
        inward = [
            remote(given(c), relay.at[1, at(c)], own_send, inner_recv, c, {"level": cross})
            for c in range(chunks)
        ]
        swaps = [
            remote(relay.at[0, at(c)], arrived.at[at(c)], outer_pass, row_recv, c, {"level": cross})
            for c in range(chunks)
        ]
        passes = [
            remote(relay.at[1, at(c)], arrived.at[at(c)], inner_pass, row_recv, c, {"level": beside})
            for c in range(chunks)
        ]

        @pl.when(inner == 0)
        def _():
            for copy in outward:
                copy.start()

        @pl.when(inner == 1)
        def _():
            for copy in inward[:2]:
                copy.start()
    else:
        swaps = [
            remote(given(c), arrived.at[at(c)], own_send, row_recv, c, {"level": other})
            for c in range(chunks)
        ]
        for copy in swaps:
            copy.start()

    left = sketch_ref[which, :, :RANK].astype(F32)
    right = sketch_ref[which, :, RANK:].astype(F32)
    with_kept = jnp.where(upper == 1, right, left).astype(BF16)
    with_arrived = jnp.where(upper == 1, left, right).astype(BF16)
    keep.wait()

    firsts, seconds, thirds = [], [], []

    def relay_on(c):
        @pl.when(inner == 1)
        def _():
            outward[c].wait_recv()
            swaps[c].start()
            if c + 2 < chunks:
                inward[c + 2].start()
            inward[c].wait_recv()
            passes[c].start()

    def compute(c):
        swaps[c].wait_recv()
        for b in range(c * group, (c + 1) * group):
            block = slice(b * RANK, (b + 1) * RANK)
            z = jnp.dot(with_kept, kept[block, :], preferred_element_type=F32)
            z = z + jnp.dot(with_arrived, arrived[block, :], preferred_element_type=F32)
            z_ref[b] = z
            high, low = split(z)
            high, low = high.astype(BF16), low.astype(BF16)
            part[b] = lax.dot_general(
                jnp.concatenate((high, low, high, low), axis=1),
                jnp.concatenate((high, high, low, low), axis=1),
                (((1,), (1,)), ((), ())), preferred_element_type=F32,
            )
        copy = remote(
            part.at[pl.ds(c * group + (1 - core) * half, half)], first.at[pl.ds(c * half, half)],
            first_send, first_recv, c, {"sample": mate},
        )
        copy.start()
        firsts.append(copy)

    def add_first(c):
        firsts[c].wait_recv()
        for b in range(half):
            partial[c * half + b] = part[c * group + core * half + b] + first[c * half + b]
        copy = remote(
            partial.at[pl.ds(c * half, half)], second.at[pl.ds(c * half, half)],
            second_send, second_recv, c, {"sample": across},
        )
        copy.start()
        seconds.append(copy)

    def add_second(c):
        seconds[c].wait_recv()
        for b in range(half):
            gram_ref[c * group + core * half + b] = partial[c * half + b] + second[c * half + b]
        copy = remote(
            gram_ref.at[pl.ds(c * group + core * half, half)], third.at[pl.ds(c * half, half)],
            third_send, third_recv, c, {"sample": mate},
        )
        copy.start()
        thirds.append(copy)

    def take_third(c):
        thirds[c].wait_recv()
        for b in range(half):
            gram_ref[c * group + (1 - core) * half + b] = third[c * half + b]

    stages = (compute, add_first, add_second, take_third)
    if relayed:
        stages = (relay_on,) + stages
    for step in range(chunks + len(stages) - 1):
        for depth, stage in enumerate(stages):
            if 0 <= step - depth < chunks:
                stage(step - depth)
    for copy in firsts + seconds + thirds:
        copy.wait_send()
    if relayed:
        for copy in outward:
            copy.wait_send()

        @pl.when(inner == 1)
        def _():
            for copy in swaps + passes:
                copy.wait_send()
    else:
        for copy in swaps:
            copy.wait_send()


def project(rows, sketch, which, distance, group, relayed):
    count, columns = rows.shape[0] // 2, rows.shape[1]
    boxes = count // RANK
    chunks = boxes // group
    square = (RANK, RANK)
    vmem = pl.BlockSpec(memory_space=pltpu.VMEM)
    half = pltpu.VMEM((boxes // 2,) + square, F32)
    return pl.pallas_call(
        functools.partial(project_kernel, which, distance, group, relayed),
        out_shape=(
            jax.ShapeDtypeStruct((boxes, RANK, columns), F32),
            jax.ShapeDtypeStruct((boxes,) + square, F32),
        ),
        in_specs=[pl.BlockSpec(memory_space=pltpu.HBM), vmem],
        out_specs=(vmem, vmem),
        scratch_shapes=[
            pltpu.VMEM((count, columns), BF16),
            pltpu.VMEM((2, count if relayed else 16, columns), BF16),
            pltpu.VMEM((count, columns), BF16),
            pltpu.VMEM((boxes,) + square, F32),
            half, half, half, half,
            pltpu.SemaphoreType.DMA,
        ] + [pltpu.SemaphoreType.DMA((chunks,))] * 12,
        compiler_params=pltpu.CompilerParams(
            collective_id=which, has_side_effects=True, vmem_limit_bytes=40 * 2**20
        ),
    )(rows, sketch)


def factor_kernel(gram_ref, z_ref, factor_ref, rows_ref, work, done):
    boxes, order, _ = gram_ref.shape
    strip = 4 * PANEL
    lane = lax.broadcasted_iota(jnp.int32, (PANEL, 128), 1)
    row = lax.broadcasted_iota(jnp.int32, (PANEL, 128), 0)
    box_of = lane // PANEL
    unit = (lane % PANEL == row).astype(F32)
    zeros = jnp.zeros((PANEL, 128), F32)
    picks = [box_of * PANEL + k for k in range(PANEL)]
    tiles = range(4)

    work[:, :, :order] = gram_ref[...]
    work[:, :, order:] = z_ref[...]

    def across_rows(value, j):
        return jnp.broadcast_to(value[j:j + 1, :], value.shape)

    def turn(value, groups):
        shift = groups * PANEL % 128
        return pltpu.roll(value, shift, axis=1) if shift else value

    def strip_inverse(top):
        grid = [[unit if a == c else zeros for c in tiles] for a in tiles]
        for a in tiles:
            for m in range(boxes):
                old = work[m, top + a * PANEL:top + (a + 1) * PANEL, :order]
                for c in tiles:
                    moved = turn(old, m - top // PANEL - c)
                    grid[a][c] = jnp.where(box_of == m, moved, grid[a][c])
        for b in tiles:
            rest = range(b, 4)
            column = {
                (a, k): jnp.take_along_axis(grid[a][b], picks[k], axis=1)
                for a in rest for k in range(PANEL)
            }
            for a in rest:
                grid[a][b] = unit if a == b else zeros
            for j in range(PANEL):
                scale = lax.rsqrt(across_rows(column[b, j], j))
                below = {a: column[a, j] * scale for a in rest}
                for k in range(j + 1, PANEL):
                    solved = across_rows(column[b, k], j) * scale
                    for a in rest:
                        column[a, k] = column[a, k] - below[a] * solved
                for c in tiles:
                    solved = across_rows(grid[b][c], j) * scale
                    for a in rest:
                        new = grid[a][c] - below[a] * solved
                        if a == b:
                            new = jnp.where(row > j, new, jnp.where(row == j, solved, grid[a][c]))
                        grid[a][c] = new
        return grid

    for top in range(0, order, strip):
        grid = strip_inverse(top)
        panels = []
        for m in range(boxes):
            pieces = []
            for a in tiles:
                piece = zeros
                for c in range(a + 1):
                    piece = jnp.where(box_of == c, turn(grid[a][c], c - m), piece)
                pieces.append(piece)
            inverse = jnp.concatenate(pieces, axis=0)[:, :strip]
            high, low = split(inverse)
            left = jnp.concatenate((high, low), axis=0).astype(BF16)
            high, low = split(work[m, top:top + strip, :])
            right = jnp.concatenate((high, low), axis=1).astype(BF16)
            terms = jnp.dot(left, right, preferred_element_type=F32)
            wide = terms.shape[1] // 2
            new = terms[:strip, :wide] + (
                terms[strip:, :wide] + terms[:strip, wide:] + terms[strip:, wide:]
            )
            done[m, top:top + strip, :] = new
            panels.append(new)
        if top + strip < order:
            for m in range(boxes):
                high, low = split(panels[m])
                right = jnp.concatenate((high, high, low, low), axis=0).astype(BF16)
                left = jnp.concatenate((high, low, high, low), axis=0)[:, :order]
                left = left.T[top + strip:, :].astype(BF16)
                work[m, top + strip:, :] = work[m, top + strip:, :] - jnp.dot(
                    left, right, preferred_element_type=F32
                )

    keep = lax.broadcasted_iota(jnp.int32, (order, order), 0) >= lax.broadcasted_iota(
        jnp.int32, (order, order), 1
    )
    for m in range(boxes):
        factor_ref[m] = jnp.where(keep, done[m, :, :order].T, 0.0)
        rows_ref[m] = (done[m, :, order:] * math.sqrt(SAMPLES)).astype(rows_ref.dtype)


def factor(gram, z, dtype):
    boxes, order, columns = z.shape
    together = min(16, boxes)
    spec = pl.BlockSpec((together, order, order), lambda i: (i, 0, 0))
    wide = pl.BlockSpec((together, order, columns), lambda i: (i, 0, 0))
    factors, rows = pl.pallas_call(
        factor_kernel,
        grid=(boxes // together,),
        out_shape=(
            jax.ShapeDtypeStruct((boxes, order, order), F32),
            jax.ShapeDtypeStruct((boxes, order, columns), dtype),
        ),
        in_specs=[spec, wide],
        out_specs=(spec, wide),
        scratch_shapes=[pltpu.VMEM((together, order, order + columns), F32)] * 2,
        compiler_params=pltpu.CompilerParams(vmem_limit_bytes=40 * 2**20),
    )(gram, z)
    return factors, rows.reshape(boxes * order, columns)


def shards(samples, sketch):
    far = lax.axis_size("level") // 2
    z, gram = project(samples, sketch, 0, far, 2, far >= 2)
    far_factors, first_rows = factor(gram, z, BF16)
    z, gram = project(first_rows, sketch, 1, 1, 2, False)
    near_factors, basis_rows = factor(gram, z, F32)
    return (far_factors, near_factors, basis_rows)


def solution(mesh):
    return jax.shard_map(
        shards,
        mesh=mesh,
        in_specs=(P("level", "sample"), P()),
        out_specs=(P("level", None, None), P("level", None, None), P("level", "sample")),
        check_vma=False,
    )
```

profile of v0, /device:TPU:0, one launch (start us, length us, event | category | flops | bytes accessed | tf_op | source)
XLA Modules:
  0.0 71.1 jit_solution(8914772386311667323)
XLA Ops:
  0.6 0.0 copy-start
  0.6 1.2 %copy-done = bf16[4096,128]{1,0:T(8,128)(2,1)S(1)} copy-done((bf16[4096,128]{1,0:T(8,128)(2,1)S(1)}, bf16[4096,128]{1,0:T(8,128)(2,1)}, u32[]{:S(2)}) %copy-start) | copy-done | bytes 1048600
  1.9 0.0 copy-start.1
  1.9 0.9 %copy-done.1 = bf16[2,128,256]{2,1,0:T(8,128)(2,1)S(1)} copy-done((bf16[2,128,256]{2,1,0:T(8,128)(2,1)S(1)}, bf16[2,128,256]{2,1,0:T(8,128)(2,1)}, u32[]{:S(2)}) %copy-start.1) | copy-done | bytes 131096
  2.8 37.8 %shard_map.49 = (f32[16,128,128]{2,1,0:T(8,128)S(1)}, f32[16,128,128]{2,1,0:T(8,128)S(1)}) custom-call(bf16[4096,128]{1,0:T(8,128)(2,1)S(1)} %copy-done, bf16[2,128,256]{2,1,0:T(8,128)(2,1)S(1)} %copy-done.1), custom_call_target="tpu_custom_call" | custom-call | tf_op jit(solution)/shard_map/pallas_call | solution.py:201
  40.6 0.0 copy-start.2
  40.6 6.9 %shard_map.50 = (f32[16,128,128]{2,1,0:T(8,128)}, bf16[16,128,128]{2,1,0:T(8,128)(2,1)S(1)}) custom-call(f32[16,128,128]{2,1,0:T(8,128)S(1)} %get-tuple-element.11.gram_ref, f32[16,128,128]{2,1,0:T(8,128)S(1)} %get-tuple-element.12.z_ref), custom_call_target="tpu_custom_call" | custom-call | tf_op jit(solution)/shard_map/pallas_call | solution.py:321
  47.5 0.0 copy-done.2
  47.5 17.0 %shard_map.51 = (f32[8,128,128]{2,1,0:T(8,128)S(1)}, f32[8,128,128]{2,1,0:T(8,128)S(1)}) custom-call(bf16[2048,128]{1,0:T(8,128)(2,1)S(1)} %bitcast.2, bf16[2,128,256]{2,1,0:T(8,128)(2,1)S(1)} %copy-done.2), custom_call_target="tpu_custom_call" | custom-call | tf_op jit(solution)/shard_map/pallas_call | solution.py:201
  64.6 6.6 %shard_map.52 = (f32[8,128,128]{2,1,0:T(8,128)}, f32[8,128,128]{2,1,0:T(8,128)}) custom-call(f32[8,128,128]{2,1,0:T(8,128)S(1)} %get-tuple-element.15.gram_ref, f32[8,128,128]{2,1,0:T(8,128)S(1)} %get-tuple-element.16.z_ref), custom_call_target="tpu_custom_call" | custom-call | tf_op jit(solution)/shard_map/pallas_call | solution.py:321
Async XLA Ops:
  0.6 1.2 %copy-start = (bf16[4096,128]{1,0:T(8,128)(2,1)S(1)}, bf16[4096,128]{1,0:T(8,128)(2,1)}, u32[]{:S(2)}) copy-start(bf16[4096,128]{1,0:T(8,128)(2,1)} %rows_ref.1) | copy-start | bytes 3145732
  1.9 0.9 %copy-start.1 = (bf16[2,128,256]{2,1,0:T(8,128)(2,1)S(1)}, bf16[2,128,256]{2,1,0:T(8,128)(2,1)}, u32[]{:S(2)}) copy-start(bf16[2,128,256]{2,1,0:T(8,128)(2,1)} %sketch_ref.3) | copy-start | bytes 393220
  40.6 6.9 %copy-start.2 = (bf16[2,128,256]{2,1,0:T(8,128)(2,1)S(1)}, bf16[2,128,256]{2,1,0:T(8,128)(2,1)}, u32[]{:S(2)}) copy-start(bf16[2,128,256]{2,1,0:T(8,128)(2,1)} %sketch_ref.3) | copy-start | bytes 393220
where the time goes:
time: 71.3 us; the launch traced here: 71.1 us
  Pallas kernels  68.3 us (96%)
  local copies, waits for them, and re-layouts  2.13 us (3%)
    pallas_call x2, Pallas kernels, project(): pl.pallas_call(functools.partial(project_kernel, which, distance, group,...  54.8 us
    pallas_call x2, Pallas kernels, factor(): pl.pallas_call(factor_kernel, grid=(boxes // together,), out_shape=(jax.S...  13.5 us
    unnamed x6, local copies, waits for them, and re-layouts  2.13 us

commit v1 on v0

--- a/solution.py
+++ b/solution.py
@@ -11,6 +11,7 @@
 SAMPLES = 512
 RANK = 128
 PANEL = 8
+PACKED = 72
 F32 = jnp.float32
 BF16 = jnp.bfloat16
 
@@ -18,6 +19,36 @@
 def split(value):
     high = value.astype(BF16).astype(F32)
     return high, value - high
+
+
+def pack_masks():
+    side = RANK // 2
+    lane = lax.broadcasted_iota(jnp.int32, (side, RANK), 1)
+    row = lax.broadcasted_iota(jnp.int32, (side, RANK), 0)
+    return lane < side, row - lane % side
+
+
+def pack(gram):
+    side = RANK // 2
+    first, below = pack_masks()
+    top, bottom = gram[:side, :], gram[side:, :]
+    main = jnp.where(first == (below >= 0), top, bottom)
+    middle = jnp.where(below == 0, jnp.where(first, bottom, top), 0.0)
+    middle = jnp.sum(middle, axis=0, keepdims=True)
+    return jnp.concatenate((main, jnp.broadcast_to(middle, (PACKED - side, RANK))), axis=0)
+
+
+def unpack(packed):
+    side = RANK // 2
+    first, below = pack_masks()
+    main = packed[:side, :]
+    middle = jnp.broadcast_to(packed[side:side + 1, :], main.shape)
+    turned = jnp.concatenate((main, main), axis=0).T
+    lower = jnp.where(below == 0, middle, turned[:side, :])
+    upper = jnp.where(below == 0, middle, turned[side:, :])
+    top = jnp.where(first, jnp.where(below >= 0, main, turned[:side, :]), jnp.where(below < 0, main, lower))
+    bottom = jnp.where(first, jnp.where(below < 0, main, upper), jnp.where(below >= 0, main, turned[side:, :]))
+    return jnp.concatenate((top, bottom), axis=0)
 
 
 def project_kernel(
@@ -130,11 +161,12 @@
             z_ref[b] = z
             high, low = split(z)
             high, low = high.astype(BF16), low.astype(BF16)
-            part[b] = lax.dot_general(
+            gram = lax.dot_general(
                 jnp.concatenate((high, low, high, low), axis=1),
                 jnp.concatenate((high, high, low, low), axis=1),
                 (((1,), (1,)), ((), ())), preferred_element_type=F32,
             )
+            part[b] = pack(gram)
         copy = remote(
             part.at[pl.ds(c * group + (1 - core) * half, half)], first.at[pl.ds(c * half, half)],
             first_send, first_recv, c, {"sample": mate},
@@ -195,7 +227,7 @@
     count, columns = rows.shape[0] // 2, rows.shape[1]
     boxes = count // RANK
     chunks = boxes // group
-    square = (RANK, RANK)
+    square = (PACKED, RANK)
     vmem = pl.BlockSpec(memory_space=pltpu.VMEM)
     half = pltpu.VMEM((boxes // 2,) + square, F32)
     return pl.pallas_call(
@@ -221,7 +253,7 @@
 
 
 def factor_kernel(gram_ref, z_ref, factor_ref, rows_ref, work, done):
-    boxes, order, _ = gram_ref.shape
+    boxes, order = z_ref.shape[:2]
     strip = 4 * PANEL
     lane = lax.broadcasted_iota(jnp.int32, (PANEL, 128), 1)
     row = lax.broadcasted_iota(jnp.int32, (PANEL, 128), 0)
@@ -231,7 +263,8 @@
     picks = [box_of * PANEL + k for k in range(PANEL)]
     tiles = range(4)
 
-    work[:, :, :order] = gram_ref[...]
+    for m in range(boxes):
+        work[m, :, :order] = unpack(gram_ref[m])
     work[:, :, order:] = z_ref[...]
 
     def across_rows(value, j):
@@ -325,7 +358,7 @@
             jax.ShapeDtypeStruct((boxes, order, order), F32),
             jax.ShapeDtypeStruct((boxes, order, columns), dtype),
         ),
-        in_specs=[spec, wide],
+        in_specs=[pl.BlockSpec((together,) + gram.shape[1:], lambda i: (i, 0, 0)), wide],
         out_specs=(spec, wide),
         scratch_shapes=[pltpu.VMEM((together, order, order + columns), F32)] * 2,
         compiler_params=pltpu.CompilerParams(vmem_limit_bytes=40 * 2**20),

time: 71.3 us -> 69.3 us (0.972)
  Pallas kernels: 68.3 us -> 66.4 us
    pallas_call x2, Pallas kernels: 54.8 us -> 52.3 us  [project(): pl.pallas_call(functools.partial(project_kernel, which, distance, group,...]
where the time goes in v1:
time: 69.3 us; the launch traced here: 69.2 us
  Pallas kernels  66.4 us (96%)
  local copies, waits for them, and re-layouts  2.13 us (3%)
    pallas_call x2, Pallas kernels, project(): pl.pallas_call(functools.partial(project_kernel, which, distance, group,...  52.3 us
    pallas_call x2, Pallas kernels, factor(): pl.pallas_call(factor_kernel, grid=(boxes // together,), out_shape=(jax.S...  14.1 us
    unnamed x6, local copies, waits for them, and re-layouts  2.13 us

profile of v1, /device:TPU:0, one launch (start us, length us, event | category | flops | bytes accessed | tf_op | source)
XLA Modules:
  0.0 69.2 jit_solution(4810814660994598072)
XLA Ops:
  0.6 0.0 copy-start
  0.6 1.2 %copy-done = bf16[4096,128]{1,0:T(8,128)(2,1)S(1)} copy-done((bf16[4096,128]{1,0:T(8,128)(2,1)S(1)}, bf16[4096,128]{1,0:T(8,128)(2,1)}, u32[]{:S(2)}) %copy-start) | copy-done | bytes 1048600
  1.9 0.0 copy-start.1
  1.9 0.9 %copy-done.1 = bf16[2,128,256]{2,1,0:T(8,128)(2,1)S(1)} copy-done((bf16[2,128,256]{2,1,0:T(8,128)(2,1)S(1)}, bf16[2,128,256]{2,1,0:T(8,128)(2,1)}, u32[]{:S(2)}) %copy-start.1) | copy-done | bytes 131096
  2.8 36.4 %shard_map.49 = (f32[16,128,128]{2,1,0:T(8,128)S(1)}, f32[16,72,128]{2,1,0:T(8,128)S(1)}) custom-call(bf16[4096,128]{1,0:T(8,128)(2,1)S(1)} %copy-done, bf16[2,128,256]{2,1,0:T(8,128)(2,1)S(1)} %copy-done.1), custom_call_target="tpu_custom_call" | custom-call | tf_op jit(solution)/shard_map/pallas_call | solution.py:233
  39.1 0.0 copy-start.2
  39.1 7.3 %shard_map.50 = (f32[16,128,128]{2,1,0:T(8,128)}, bf16[16,128,128]{2,1,0:T(8,128)(2,1)S(1)}) custom-call(f32[16,72,128]{2,1,0:T(8,128)S(1)} %get-tuple-element.11.gram_ref, f32[16,128,128]{2,1,0:T(8,128)S(1)} %get-tuple-element.12.z_ref), custom_call_target="tpu_custom_call" | custom-call | tf_op jit(solution)/shard_map/pallas_call | solution.py:354
  46.4 0.0 copy-done.2
  46.4 15.9 %shard_map.51 = (f32[8,128,128]{2,1,0:T(8,128)S(1)}, f32[8,72,128]{2,1,0:T(8,128)S(1)}) custom-call(bf16[2048,128]{1,0:T(8,128)(2,1)S(1)} %bitcast.2, bf16[2,128,256]{2,1,0:T(8,128)(2,1)S(1)} %copy-done.2), custom_call_target="tpu_custom_call" | custom-call | tf_op jit(solution)/shard_map/pallas_call | solution.py:233
  62.4 6.8 %shard_map.52 = (f32[8,128,128]{2,1,0:T(8,128)}, f32[8,128,128]{2,1,0:T(8,128)}) custom-call(f32[8,72,128]{2,1,0:T(8,128)S(1)} %get-tuple-element.15.gram_ref, f32[8,128,128]{2,1,0:T(8,128)S(1)} %get-tuple-element.16.z_ref), custom_call_target="tpu_custom_call" | custom-call | tf_op jit(solution)/shard_map/pallas_call | solution.py:354
Async XLA Ops:
  0.6 1.2 %copy-start = (bf16[4096,128]{1,0:T(8,128)(2,1)S(1)}, bf16[4096,128]{1,0:T(8,128)(2,1)}, u32[]{:S(2)}) copy-start(bf16[4096,128]{1,0:T(8,128)(2,1)} %rows_ref.1) | copy-start | bytes 3145732
  1.9 0.9 %copy-start.1 = (bf16[2,128,256]{2,1,0:T(8,128)(2,1)S(1)}, bf16[2,128,256]{2,1,0:T(8,128)(2,1)}, u32[]{:S(2)}) copy-start(bf16[2,128,256]{2,1,0:T(8,128)(2,1)} %sketch_ref.3) | copy-start | bytes 393220
  39.1 7.3 %copy-start.2 = (bf16[2,128,256]{2,1,0:T(8,128)(2,1)S(1)}, bf16[2,128,256]{2,1,0:T(8,128)(2,1)}, u32[]{:S(2)}) copy-start(bf16[2,128,256]{2,1,0:T(8,128)(2,1)} %sketch_ref.3) | copy-start | bytes 393220

commit v2 on v1

--- a/solution.py
+++ b/solution.py
@@ -68,6 +68,7 @@
     chunks = boxes // group
     half = group // 2
     size = group * RANK
+    ahead = min(4, chunks)
     if relayed:
         hop = distance // 2
         place = level // hop % 4
@@ -124,7 +125,7 @@
 
         @pl.when(inner == 1)
         def _():
-            for copy in inward[:2]:
+            for copy in inward[:ahead]:
                 copy.start()
     else:
         swaps = [
@@ -147,8 +148,8 @@
         def _():
             outward[c].wait_recv()
             swaps[c].start()
-            if c + 2 < chunks:
-                inward[c + 2].start()
+            if c + ahead < chunks:
+                inward[c + ahead].start()
             inward[c].wait_recv()
             passes[c].start()
 
@@ -201,11 +202,11 @@
         for b in range(half):
             gram_ref[c * group + (1 - core) * half + b] = third[c * half + b]
 
-    stages = (compute, add_first, add_second, take_third)
+    stages = [(0, compute), (1, add_first), (2, add_second), (3, take_third)]
     if relayed:
-        stages = (relay_on,) + stages
-    for step in range(chunks + len(stages) - 1):
-        for depth, stage in enumerate(stages):
+        stages = [(0, relay_on)] + [(depth + ahead - 1, stage) for depth, stage in stages]
+    for step in range(chunks + stages[-1][0]):
+        for depth, stage in stages:
             if 0 <= step - depth < chunks:
                 stage(step - depth)
     for copy in firsts + seconds + thirds:
@@ -290,8 +291,13 @@
             }
             for a in rest:
                 grid[a][b] = unit if a == b else zeros
+            pivot = across_rows(column[b, 0], 0)
             for j in range(PANEL):
-                scale = lax.rsqrt(across_rows(column[b, j], j))
+                scale = lax.rsqrt(pivot)
+                if j + 1 < PANEL:
+                    pivot = across_rows(column[b, j + 1], j + 1) - (
+                        across_rows(column[b, j], j + 1) * scale
+                    ) * (across_rows(column[b, j + 1], j) * scale)
                 below = {a: column[a, j] * scale for a in rest}
                 for k in range(j + 1, PANEL):
                     solved = across_rows(column[b, k], j) * scale

time: 69.3 us -> 67.4 us (0.973)
  the two profiles are of different devices: /device:TPU:0 before, /device:TPU:9 now
where the time goes in v2:
time: 67.4 us; the launch traced here: 67.2 us
  Pallas kernels  64.4 us (96%)
  local copies, waits for them, and re-layouts  2.13 us (3%)
    pallas_call x2, Pallas kernels, project(): pl.pallas_call(functools.partial(project_kernel, which, distance, group,...  50.9 us
    pallas_call x2, Pallas kernels, factor(): pl.pallas_call(factor_kernel, grid=(boxes // together,), out_shape=(jax.S...  13.6 us
    unnamed x6, local copies, waits for them, and re-layouts  2.13 us

profile of v2, /device:TPU:9, one launch (start us, length us, event | category | flops | bytes accessed | tf_op | source)
XLA Modules:
  0.0 67.2 jit_solution(17775101732294710242)
XLA Ops:
  0.6 0.0 copy-start
  0.6 1.2 %copy-done = bf16[4096,128]{1,0:T(8,128)(2,1)S(1)} copy-done((bf16[4096,128]{1,0:T(8,128)(2,1)S(1)}, bf16[4096,128]{1,0:T(8,128)(2,1)}, u32[]{:S(2)}) %copy-start) | copy-done | bytes 1048600
  1.9 0.0 copy-start.1
  1.9 0.9 %copy-done.1 = bf16[2,128,256]{2,1,0:T(8,128)(2,1)S(1)} copy-done((bf16[2,128,256]{2,1,0:T(8,128)(2,1)S(1)}, bf16[2,128,256]{2,1,0:T(8,128)(2,1)}, u32[]{:S(2)}) %copy-start.1) | copy-done | bytes 131096
  2.8 35.5 %shard_map.49 = (f32[16,128,128]{2,1,0:T(8,128)S(1)}, f32[16,72,128]{2,1,0:T(8,128)S(1)}) custom-call(bf16[4096,128]{1,0:T(8,128)(2,1)S(1)} %copy-done, bf16[2,128,256]{2,1,0:T(8,128)(2,1)S(1)} %copy-done.1), custom_call_target="tpu_custom_call" | custom-call | tf_op jit(solution)/shard_map/pallas_call | solution.py:234
  38.3 0.0 copy-start.2
  38.3 7.1 %shard_map.50 = (f32[16,128,128]{2,1,0:T(8,128)}, bf16[16,128,128]{2,1,0:T(8,128)(2,1)S(1)}) custom-call(f32[16,72,128]{2,1,0:T(8,128)S(1)} %get-tuple-element.11.gram_ref, f32[16,128,128]{2,1,0:T(8,128)S(1)} %get-tuple-element.12.z_ref), custom_call_target="tpu_custom_call" | custom-call | tf_op jit(solution)/shard_map/pallas_call | solution.py:360
  45.4 0.0 copy-done.2
  45.4 15.4 %shard_map.51 = (f32[8,128,128]{2,1,0:T(8,128)S(1)}, f32[8,72,128]{2,1,0:T(8,128)S(1)}) custom-call(bf16[2048,128]{1,0:T(8,128)(2,1)S(1)} %bitcast.2, bf16[2,128,256]{2,1,0:T(8,128)(2,1)S(1)} %copy-done.2), custom_call_target="tpu_custom_call" | custom-call | tf_op jit(solution)/shard_map/pallas_call | solution.py:234
  60.8 6.4 %shard_map.52 = (f32[8,128,128]{2,1,0:T(8,128)}, f32[8,128,128]{2,1,0:T(8,128)}) custom-call(f32[8,72,128]{2,1,0:T(8,128)S(1)} %get-tuple-element.15.gram_ref, f32[8,128,128]{2,1,0:T(8,128)S(1)} %get-tuple-element.16.z_ref), custom_call_target="tpu_custom_call" | custom-call | tf_op jit(solution)/shard_map/pallas_call | solution.py:360
Async XLA Ops:
  0.6 1.2 %copy-start = (bf16[4096,128]{1,0:T(8,128)(2,1)S(1)}, bf16[4096,128]{1,0:T(8,128)(2,1)}, u32[]{:S(2)}) copy-start(bf16[4096,128]{1,0:T(8,128)(2,1)} %rows_ref.1) | copy-start | bytes 3145732
  1.9 0.9 %copy-start.1 = (bf16[2,128,256]{2,1,0:T(8,128)(2,1)S(1)}, bf16[2,128,256]{2,1,0:T(8,128)(2,1)}, u32[]{:S(2)}) copy-start(bf16[2,128,256]{2,1,0:T(8,128)(2,1)} %sketch_ref.3) | copy-start | bytes 393220
  38.3 7.1 %copy-start.2 = (bf16[2,128,256]{2,1,0:T(8,128)(2,1)S(1)}, bf16[2,128,256]{2,1,0:T(8,128)(2,1)}, u32[]{:S(2)}) copy-start(bf16[2,128,256]{2,1,0:T(8,128)(2,1)} %sketch_ref.3) | copy-start | bytes 393220

commit v3 on v2

--- a/solution.py
+++ b/solution.py
@@ -68,7 +68,7 @@
     chunks = boxes // group
     half = group // 2
     size = group * RANK
-    ahead = min(4, chunks)
+    ahead = min(3, chunks)
     if relayed:
         hop = distance // 2
         place = level // hop % 4
@@ -132,7 +132,7 @@
             remote(given(c), arrived.at[at(c)], own_send, row_recv, c, {"level": other})
             for c in range(chunks)
         ]
-        for copy in swaps:
+        for copy in swaps[:2]:
             copy.start()
 
     left = sketch_ref[which, :, :RANK].astype(F32)
@@ -155,6 +155,8 @@
 
     def compute(c):
         swaps[c].wait_recv()
+        if not relayed and c + 2 < chunks:
+            swaps[c + 2].start()
         for b in range(c * group, (c + 1) * group):
             block = slice(b * RANK, (b + 1) * RANK)
             z = jnp.dot(with_kept, kept[block, :], preferred_element_type=F32)
@@ -204,7 +206,7 @@
 
     stages = [(0, compute), (1, add_first), (2, add_second), (3, take_third)]
     if relayed:
-        stages = [(0, relay_on)] + [(depth + ahead - 1, stage) for depth, stage in stages]
+        stages = [(0, relay_on)] + [(depth + 3, stage) for depth, stage in stages]
     for step in range(chunks + stages[-1][0]):
         for depth, stage in stages:
             if 0 <= step - depth < chunks:

time: 67.4 us -> 68.8 us (1.021)
  the two profiles are of different devices: /device:TPU:9 before, /device:TPU:0 now
where the time goes in v3:
time: 68.8 us; the launch traced here: 67.7 us
  Pallas kernels  64.9 us (94%)
  local copies, waits for them, and re-layouts  2.13 us (3%)
    pallas_call x2, Pallas kernels, project(): pl.pallas_call(functools.partial(project_kernel, which, distance, group,...  51.4 us
    pallas_call x2, Pallas kernels, factor(): pl.pallas_call(factor_kernel, grid=(boxes // together,), out_shape=(jax.S...  13.6 us
    unnamed x6, local copies, waits for them, and re-layouts  2.13 us

profile of v3, /device:TPU:0, one launch (start us, length us, event | category | flops | bytes accessed | tf_op | source)
XLA Modules:
  0.0 67.7 jit_solution(1910525867121299225)
XLA Ops:
  0.6 0.0 copy-start
  0.6 1.2 %copy-done = bf16[4096,128]{1,0:T(8,128)(2,1)S(1)} copy-done((bf16[4096,128]{1,0:T(8,128)(2,1)S(1)}, bf16[4096,128]{1,0:T(8,128)(2,1)}, u32[]{:S(2)}) %copy-start) | copy-done | bytes 1048600
  1.9 0.0 copy-start.1
  1.9 0.9 %copy-done.1 = bf16[2,128,256]{2,1,0:T(8,128)(2,1)S(1)} copy-done((bf16[2,128,256]{2,1,0:T(8,128)(2,1)S(1)}, bf16[2,128,256]{2,1,0:T(8,128)(2,1)}, u32[]{:S(2)}) %copy-start.1) | copy-done | bytes 131096
  2.8 34.6 %shard_map.49 = (f32[16,128,128]{2,1,0:T(8,128)S(1)}, f32[16,72,128]{2,1,0:T(8,128)S(1)}) custom-call(bf16[4096,128]{1,0:T(8,128)(2,1)S(1)} %copy-done, bf16[2,128,256]{2,1,0:T(8,128)(2,1)S(1)} %copy-done.1), custom_call_target="tpu_custom_call" | custom-call | tf_op jit(solution)/shard_map/pallas_call | solution.py:236
  37.4 0.0 copy-start.2
  37.4 7.1 %shard_map.50 = (f32[16,128,128]{2,1,0:T(8,128)}, bf16[16,128,128]{2,1,0:T(8,128)(2,1)S(1)}) custom-call(f32[16,72,128]{2,1,0:T(8,128)S(1)} %get-tuple-element.11.gram_ref, f32[16,128,128]{2,1,0:T(8,128)S(1)} %get-tuple-element.12.z_ref), custom_call_target="tpu_custom_call" | custom-call | tf_op jit(solution)/shard_map/pallas_call | solution.py:362
  44.5 0.0 copy-done.2
  44.5 16.8 %shard_map.51 = (f32[8,128,128]{2,1,0:T(8,128)S(1)}, f32[8,72,128]{2,1,0:T(8,128)S(1)}) custom-call(bf16[2048,128]{1,0:T(8,128)(2,1)S(1)} %bitcast.2, bf16[2,128,256]{2,1,0:T(8,128)(2,1)S(1)} %copy-done.2), custom_call_target="tpu_custom_call" | custom-call | tf_op jit(solution)/shard_map/pallas_call | solution.py:236
  61.3 6.4 %shard_map.52 = (f32[8,128,128]{2,1,0:T(8,128)}, f32[8,128,128]{2,1,0:T(8,128)}) custom-call(f32[8,72,128]{2,1,0:T(8,128)S(1)} %get-tuple-element.15.gram_ref, f32[8,128,128]{2,1,0:T(8,128)S(1)} %get-tuple-element.16.z_ref), custom_call_target="tpu_custom_call" | custom-call | tf_op jit(solution)/shard_map/pallas_call | solution.py:362
Async XLA Ops:
  0.6 1.2 %copy-start = (bf16[4096,128]{1,0:T(8,128)(2,1)S(1)}, bf16[4096,128]{1,0:T(8,128)(2,1)}, u32[]{:S(2)}) copy-start(bf16[4096,128]{1,0:T(8,128)(2,1)} %rows_ref.1) | copy-start | bytes 3145732
  1.9 0.9 %copy-start.1 = (bf16[2,128,256]{2,1,0:T(8,128)(2,1)S(1)}, bf16[2,128,256]{2,1,0:T(8,128)(2,1)}, u32[]{:S(2)}) copy-start(bf16[2,128,256]{2,1,0:T(8,128)(2,1)} %sketch_ref.3) | copy-start | bytes 393220
  37.4 7.1 %copy-start.2 = (bf16[2,128,256]{2,1,0:T(8,128)(2,1)S(1)}, bf16[2,128,256]{2,1,0:T(8,128)(2,1)}, u32[]{:S(2)}) copy-start(bf16[2,128,256]{2,1,0:T(8,128)(2,1)} %sketch_ref.3) | copy-start | bytes 393220
